TPU v7x, 32 devices: a whole 2x2x4 slice. The times are simulated.
32 devices in a mesh: ctx: 8 (over z, y), head: 4 (over x, core).
Axes of the slice: x: 2, y: 2, z: 4, core: 2. Of those that a mesh axis runs over, the one named last changes fastest.
Arguments:
- queries: bfloat16 [16384, 8192], P('ctx', 'head'), may hold values from -9 to 9
- keys: bfloat16 [16384, 1024], P('ctx', 'head'), may hold values from -8 to 8
- values: bfloat16 [16384, 1024], P('ctx', 'head'), may hold values from -6 to 6
- source_block: int32 [128], replicated, may hold values from 0 to 127, as said below
- doc_of_block: int32 [128], replicated, may hold values from 0 to 27, never falling along the last dimension, each value on 1 to 8 neighbouring positions
Outputs:
- attended: bfloat16 [16384, 8192], P(('ctx', 'head'))
Inputs may be any that keep to these rules, and one draw needn't show every extreme that they name: `source_block`: each number once. Generation row block b belongs to generation owner b // 16; pack block p lies on context shard p // 16; a context shard receives at most 2 blocks from one generation owner. `doc_of_block`: never falling along the pack; a rollout covers 1 to 8 blocks.
All inputs are finite; a program needn't handle non-finite values.
Results may differ from a plain program's by a relative error of at most 0.008.
Values may be sent and summed in bfloat16 or wider, within the bound.
A program may use at most 64 MiB of HBM per device.

v0:
```python
import jax
import jax.numpy as jnp
from jax import lax
from jax.sharding import PartitionSpec as P

HEAD_SIZE = 128
BLK = 128
DOCMAX = 8


def shifted(block, axis, distance):
    devices = range(lax.axis_size(axis))
    route = [(i - distance, i) for i in devices if i - distance in devices]
    return lax.ppermute(block, axis, route)


def attend(packed_queries, key_extended, value_extended, doc_ext):
    block_total = packed_queries.shape[0] // BLK
    window = DOCMAX * BLK
    key_pos = jnp.arange(window)
    query_pos = (DOCMAX - 1) * BLK + jnp.arange(BLK)
    causal = key_pos[None, :] <= query_pos[:, None]

    def one_block(block_index):
        row_start = block_index * BLK
        query_block = lax.dynamic_slice_in_dim(packed_queries, row_start, BLK, 0)
        key_window = lax.dynamic_slice_in_dim(key_extended, row_start, window, 0)
        value_window = lax.dynamic_slice_in_dim(value_extended, row_start, window, 0)
        window_docs = lax.dynamic_slice_in_dim(doc_ext, block_index, DOCMAX, 0)
        same_doc = window_docs == window_docs[DOCMAX - 1]
        allowed = causal & same_doc[key_pos // BLK][None, :]
        scores = jnp.einsum(
            "qngd,knd->ngqk", query_block, key_window, preferred_element_type=jnp.float32
        ) * HEAD_SIZE ** (-0.5)
        masked = jnp.where(allowed, scores, -1e30)
        row_max = jnp.max(masked, axis=-1, keepdims=True)
        expo_terms = jnp.where(allowed, jnp.exp(masked - row_max), 0.0)
        weights = (expo_terms / jnp.sum(expo_terms, axis=-1, keepdims=True)).astype(jnp.bfloat16)
        mixed_out = jnp.einsum(
            "ngqk,knd->qngd", weights, value_window, preferred_element_type=jnp.float32
        )
        return mixed_out.astype(jnp.bfloat16)

    stacked = lax.map(one_block, jnp.arange(block_total, dtype=jnp.int32))
    return stacked.reshape(packed_queries.shape)


def local(queries, keys, values, source_block, doc_of_block):
    shards = lax.axis_size("ctx")
    own_index = lax.axis_index("ctx")
    row_count = queries.shape[0]
    per_shard = row_count // BLK
    capacity = max(1, per_shard // shards)
    kv_heads = keys.shape[1] // HEAD_SIZE
    query_group_size = queries.shape[1] // keys.shape[1]
    owner_of = (source_block // per_shard).reshape(shards, per_shard)
    local_of = (source_block % per_shard).reshape(shards, per_shard)
    earlier = jnp.arange(per_shard)[None, :] < jnp.arange(per_shard)[:, None]
    same_owner = owner_of[:, :, None] == owner_of[:, None, :]
    rank_of = jnp.sum(same_owner & earlier[None], axis=2)
    matches = (owner_of[:, :, None] == own_index) & (
        rank_of[:, :, None] == jnp.arange(capacity)[None, None, :]
    )
    send_from = jnp.sum(jnp.where(matches, local_of[:, :, None], 0), axis=1).reshape(-1)
    send_live = jnp.any(matches, axis=1).reshape(-1)
    mine_owner = lax.dynamic_index_in_dim(owner_of, own_index, 0, keepdims=False)
    mine_rank = lax.dynamic_index_in_dim(rank_of, own_index, 0, keepdims=False)
    take_from = mine_owner * capacity + mine_rank

    def outgoing(array):
        blocks = array.reshape((per_shard, BLK) + array.shape[1:])
        picked = jnp.take(blocks, send_from, axis=0)
        live = send_live.reshape((-1,) + (1,) * (picked.ndim - 1))
        return jnp.where(live, picked, jnp.zeros((), array.dtype))

    def incoming(array):
        return jnp.take(array, take_from, axis=0).reshape((row_count,) + array.shape[2:])

    query_local = queries.reshape(row_count, kv_heads, query_group_size, HEAD_SIZE)
    key_local = keys.reshape(row_count, kv_heads, HEAD_SIZE)
    value_local = values.reshape(row_count, kv_heads, HEAD_SIZE)
    reach_blocks = DOCMAX - 1
    reachable_rows = reach_blocks * BLK
    global_block = own_index * per_shard - reach_blocks + jnp.arange(reach_blocks + per_shard)
    clipped = jnp.clip(global_block, 0, doc_of_block.shape[0] - 1)
    doc_ext = jnp.where(global_block >= 0, jnp.take(doc_of_block, clipped), -1)
    got_queries, got_keys, got_values = (
        lax.all_to_all(outgoing(query_local), "ctx", split_axis=0, concat_axis=0, tiled=True),
        lax.all_to_all(outgoing(key_local), "ctx", split_axis=0, concat_axis=0, tiled=True),
        lax.all_to_all(outgoing(value_local), "ctx", split_axis=0, concat_axis=0, tiled=True),
    )
    packed_keys = incoming(got_keys)
    packed_values = incoming(got_values)
    earlier_keys, earlier_values = shifted(
        (packed_keys[row_count - reachable_rows :], packed_values[row_count - reachable_rows :]),
        "ctx",
        1,
    )
    key_extended = jnp.concatenate([earlier_keys, packed_keys], axis=0)
    value_extended = jnp.concatenate([earlier_values, packed_values], axis=0)
    key_extended, value_extended = (key_extended, value_extended)
    result = attend(incoming(got_queries), key_extended, value_extended, doc_ext)
    flattened = result.reshape(row_count, queries.shape[1])
    return lax.all_to_all(flattened, "head", split_axis=0, concat_axis=1, tiled=True)


def solution(mesh):
    in_specs = (P("ctx", "head"), P("ctx", "head"), P("ctx", "head"), P(), P())
    out_specs = P(("ctx", "head"), None)
    return jax.shard_map(local, mesh=mesh, in_specs=in_specs, out_specs=out_specs, check_vma=False)
```

profile of v0, /device:TPU:12, one launch (start us, length us, event | category | flops | bytes accessed | tf_op | source)
XLA Modules:
  0.0 792.5 jit_solution(918653356939995517)
XLA Ops:
  7.9 29.6 %all_to_all.34 = bf16[16,128,2,128]{3,1,2,0:T(8,128)(2,1)S(1)} all-to-all(bf16[16,128,2,128]{3,1,2,0:T(8,128)(2,1)S(1)} %get-tuple-element.245), channel_id=1, replica_groups=mesh['ctx'=8,'head'=4] {'ctx'}, dimensions={0} | all-to-all | bytes 2097152 | tf_op jit(solution)/shard_map/all_to_all | solution.py:89
  37.5 5.8 all-to-all-start
  43.2 9.9 %copy.68 = bf16[256,8,16,128]{3,2,1,0:T(8,128)(2,1)} copy(bf16[256,8,16,128]{3,1,2,0:T(8,128)(2,1)} %bitcast.109) | data formatting | bytes 16777216
  53.2 8.1 %gather_fusion.5 = bf16[16,128,2,8,128]{4,3,2,1,0:T(8,128)(2,1)} fusion(bf16[16,128,2,8,128]{4,3,2,1,0:T(8,128)(2,1)} %bitcast.105, s32[1024]{0:T(1024)S(1)} %pad_clamp_fusion.2), kind=kCustom, calls=%fused_computation.clone | custom fusion | bytes 16777280 | tf_op jit(solution)/shard_map/jit(_take)/gather | solution.py:72
  61.3 7.6 select_select_fusion
  68.9 6.0 all-to-all-start.2
  86.9 176.7 %collective-permute-done.1 = bf16[896,2,128]{2,0,1:T(8,128)(2,1)S(1)} collective-permute-done((bf16[896,2,128]{2,0,1:T(8,128)(2,1)S(1)}, bf16[896,2,128]{2,0,1:T(8,128)(2,1)S(1)}, u32[]{:S(2)}, u32[]{:S(2)}) %collective-permute-start.1) | collective-permute-done | bytes 458784 | tf_op jit(solution)/shard_map/ppermute | solution.py:14
  263.7 9.6 %collective-permute-done = bf16[896,2,128]{2,0,1:T(8,128)(2,1)S(1)} collective-permute-done((bf16[896,2,128]{2,0,1:T(8,128)(2,1)S(1)}, bf16[896,2,128]{2,0,1:T(8,128)(2,1)S(1)}, u32[]{:S(2)}, u32[]{:S(2)}) %collective-permute-start) | collective-permute-done | bytes 458784 | tf_op jit(solution)/shard_map/ppermute | solution.py:14
  274.6 8.1 %gather_fusion.6 = bf16[16,128,2,8,128]{4,3,2,1,0:T(8,128)(2,1)} fusion(bf16[16,128,2,8,128]{4,3,2,1,0:T(8,128)(2,1)} %all-to-all-done.2, s32[1024]{0:T(1024)S(1)} %pad_clamp_fusion.1), kind=kCustom, calls=%fused_computation.2.clone | custom fusion | bytes 16777280 | tf_op jit(solution)/shard_map/jit(_take)/gather | solution.py:77
  282.7 7.5 broadcast_select_fusion.1
  290.2 365.1 %while.15 = (s32[]{:T(128)}, bf16[16,128,2,8,128]{4,3,2,1,0:T(8,128)(2,1)}, s32[16]{0:T(128)S(1)}, bf16[2944,2,128]{2,0,1:T(8,128)(2,1)}, s32[23]{0:T(128)S(1)},...) while((s32[]{:T(128)}, ...), condition=%wide.region_6.9_spmd.clone.clone, body=%wide.region_3.8_spmd.clone.sunk.clone | while | flops 1088984064 | bytes 22437224 | solution.py:44
  301.8 5.5 fusion.75
  307.3 4.4 fusion.76
  324.6 5.5 fusion.75
  330.1 4.4 fusion.76
  347.4 5.5 fusion.75
  353.0 4.4 fusion.76
  363.3 4.3 select_reduce_fusion.4
  370.3 5.5 fusion.75
  375.8 4.4 fusion.76
  393.1 5.5 fusion.75
  398.6 4.4 fusion.76
  415.9 5.5 fusion.75
  421.4 4.4 fusion.76
  438.7 5.5 fusion.75
  444.3 4.4 fusion.76
  461.6 5.5 fusion.75
  467.1 4.4 fusion.76
  484.4 5.5 fusion.75
  489.9 4.4 fusion.76
  507.2 5.5 fusion.75
  512.7 4.4 fusion.76
  530.0 5.5 fusion.75
  535.5 4.4 fusion.76
  552.8 5.5 fusion.75
  558.4 4.4 fusion.76
  575.7 5.5 fusion.75
  581.2 4.4 fusion.76
  598.5 5.5 fusion.75
  604.0 4.4 fusion.76
  621.3 5.5 fusion.75
  626.8 4.4 fusion.76
  644.1 5.5 fusion.75
  649.6 4.4 fusion.76
  655.3 13.3 %all_to_all.26 = bf16[4,512,2048]{2,1,0:T(8,128)(2,1)} reshape(bf16[16,128,2,8,128]{4,3,2,1,0:T(8,128)(2,1)} %get-tuple-element.162) | data formatting | bytes 16777216 | tf_op jit(solution)/shard_map/all_to_all | solution.py:104
  668.6 100.6 %all_to_all.35 = bf16[4,512,2048]{2,1,0:T(8,128)(2,1)} all-to-all(bf16[4,512,2048]{2,1,0:T(8,128)(2,1)} %all_to_all.26), channel_id=1, replica_groups=mesh['ctx'=8,'head'=4] {'head'}, dimensions={0} | all-to-all | bytes 16777216 | tf_op jit(solution)/shard_map/all_to_all | solution.py:104
  769.2 11.4 %copy.55 = bf16[512,4,2048]{0,2,1:T(8,128)(2,1)} copy(bf16[512,4,2048]{2,0,1:T(8,128)(2,1)} %bitcast.106) | data formatting | bytes 16777216 | tf_op jit(solution)/shard_map/all_to_all | solution.py:104
  780.6 11.9 %copy.56 = bf16[512,8192]{1,0:T(8,128)(2,1)} copy(bf16[512,8192]{0,1:T(8,128)(2,1)} %bitcast.107) | data formatting | bytes 16777216 | tf_op jit(solution)/shard_map/all_to_all | solution.py:104
  (241 shorter events, 178.3 us)
Async XLA Ops:
  0.0 82.4 %copy-start = (s32[128]{0:T(128)S(1)}, s32[128]{0:T(128)}, u32[]{:S(2)}) copy-start(s32[128]{0:T(128)} %param.15) | copy-start | bytes 1540
  37.5 31.4 %all-to-all-start = ((bf16[16,128,2,128]{3,1,2,0:T(8,128)(2,1)}), bf16[16,128,2,128]{3,1,2,0:T(8,128)(2,1)S(1)}, u32[]{:S(2)}, u32[]{:S(2)}) async-start(bf16[16,128,2,128]{3,1,2,0:T(8,128)(2,1)} %get-tuple-element.246), calls=%async_computation | async-start | bytes 2097152 | tf_op jit(solution)/shard_map/all_to_all | solution.py:90
  68.9 205.7 %all-to-all-start.2 = ((bf16[16,128,2,8,128]{4,3,2,1,0:T(8,128)(2,1)}), bf16[16,128,2,8,128]{4,3,2,1,0:T(8,128)(2,1)}, u32[]{:S(2)}, u32[]{:S(2)}) async-start(bf16[16,128,2,8,128]{4,3,2,1,0:T(8,128)(2,1)} %select_select_fusion), calls=%async_computation.2 | async-start | bytes 16777216 | tf_op jit(solution)/shard_map/all_to_all | solution.py:88
  78.9 184.6 %collective-permute-start.1 = (bf16[896,2,128]{2,0,1:T(8,128)(2,1)S(1)}, bf16[896,2,128]{2,0,1:T(8,128)(2,1)S(1)}, u32[]{:S(2)}, u32[]{:S(2)}) collective-permute-start(bf16[896,2,128]{2,0,1:T(8,128)(2,1)S(1)} %bitcast.112), channel_id=1, source_target_pairs={{0,4},{4,8},{8,12},{12,16},{16,20},{20,24},{24,28},{1,5},{5,9},{9,... | collective-permute-start | bytes 1376264 | tf_op jit(solution)/shard_map/ppermute | solution.py:14
  83.2 190.1 %collective-permute-start = (bf16[896,2,128]{2,0,1:T(8,128)(2,1)S(1)}, bf16[896,2,128]{2,0,1:T(8,128)(2,1)S(1)}, u32[]{:S(2)}, u32[]{:S(2)}) collective-permute-start(bf16[896,2,128]{2,0,1:T(8,128)(2,1)S(1)} %bitcast.113), channel_id=1, source_target_pairs={{0,4},{4,8},{8,12},{12,16},{16,20},{20,24},{24,28},{1,5},{5,9},{9,... | collective-permute-start | bytes 1376264 | tf_op jit(solution)/shard_map/ppermute | solution.py:14
  780.6 11.9 %copy-start.1 = (s32[128]{0:T(128)S(1)}, s32[128]{0:T(128)}, u32[]{:S(2)}) copy-start(s32[128]{0:T(128)} %param.15) | copy-start | bytes 1540
where the time goes:
time: 799 us; the launch traced here: 793 us
  waiting for transfers between devices  186 us (23%)
  matrix products  158 us (20%)
  local copies, waits for them, and re-layouts  141 us (18%)
  blocking collectives  130 us (16%)
  other arithmetic  113 us (14%)
  loops' own time  45.2 us (6%)
  starting transfers between devices  18.7 us (2%)
    ppermute x2, waiting for transfers between devices, shifted(): return lax.ppermute(block, axis, route)  186 us
    all_to_all x1, blocking collectives, local(): lax.all_to_all(flattened, 'head', split_axis=0, concat_axis=1, tiled=True)  101 us
    sub x16, matrix products, one_block(): expo_terms = jnp.where(allowed, jnp.exp(masked - row_max), 0.0)  88.4 us
    gather x48, other arithmetic, one_block(): allowed = causal & same_doc[key_pos // BLK][None, :]  78.5 us
    dot_general x16, matrix products, one_block(): jnp.einsum('ngqk,knd->qngd', weights, value_window, preferred_element_typ...  70 us
    another operation x1, loops' own time, attend(): stacked = lax.map(one_block, jnp.arange(block_total, dtype=jnp.int32))  45.2 us
    all_to_all x3, local copies, waits for them, and re-layouts, local(): lax.all_to_all(flattened, 'head', split_axis=0, concat_axis=1, tiled=True)  36.6 us
    all_to_all x1, blocking collectives, local(): lax.all_to_all(outgoing(key_local), 'ctx', split_axis=0, concat_axis=0, t...  29.6 us
  transfers between devices with their start and end apart: 4, of which 2 were waited for; matrix products, arithmetic and copies ran while one was open for 4% of the time, Pallas kernels for 0%

commit v1 on v0

v1 whole, which is shorter than its diff:
```python
import functools

import jax
import jax.numpy as jnp
from jax import lax
from jax.experimental import pallas as pl
from jax.experimental.pallas import tpu as pltpu
from jax.sharding import PartitionSpec as P

HEAD_SIZE = 128
BLK = 128
DOCMAX = 8
REACH = DOCMAX - 1
HEADS_PER_CHUNK = 2
LOOKAHEAD = 2
LOG2E = 1.4426950408889634


def kernel(dims, source_ref, doc_ref, queries, keys, values, out, *scratch):
    shards, groups, blocks, cap, kv_heads, chunks, width, kv_width, group_size = dims
    units = 2 + chunks
    scratch = list(scratch)

    def take(count):
        taken = scratch[:count]
        del scratch[:count]
        return taken

    local = take(units)
    outgoing = take(units)
    incoming = take(units)
    (key_ext, value_ext, stage, result, send_table, take_table, reach_table) = take(7)
    (load_sem, own_sem, send_sem, recv_sem, shift_send, shift_recv, out_send, out_recv) = take(8)

    me = lax.axis_index("ctx")
    my_group = lax.axis_index("head")
    quarter = blocks // groups

    def load(unit):
        if unit == 0:
            source = keys
        elif unit == 1:
            source = values
        else:
            source = queries.at[:, :, pl.ds((unit - 2) * width, width)]
        return pltpu.make_async_copy(source, local[unit], load_sem.at[unit])

    for unit in range(units):
        load(unit).start()

    barrier = pltpu.get_barrier_semaphore()

    def greet_shard(step, carry):
        pl.semaphore_signal(barrier, inc=1, device_id={"ctx": lax.rem(me + step, shards)},
                            device_id_type=pl.DeviceIdType.MESH)
        return carry

    def greet_group(step, carry):
        pl.semaphore_signal(barrier, inc=1, device_id={"head": lax.rem(my_group + step, groups)},
                            device_id_type=pl.DeviceIdType.MESH)
        return carry

    lax.fori_loop(1, shards, greet_shard, 0)
    lax.fori_loop(1, groups, greet_group, 0)

    def fill_send(shard, carry):
        picks = [jnp.int32(0)] * cap
        count = jnp.int32(0)
        for i in range(blocks):
            number = source_ref[shard * blocks + i]
            mine = lax.div(number, blocks) == me
            place = lax.rem(number, blocks)
            for r in range(cap):
                picks[r] = jnp.where(mine & (count == r), place, picks[r])
            count = count + jnp.where(mine, 1, 0)
        for r in range(cap):
            send_table[shard * cap + r] = picks[r]
        return carry

    lax.fori_loop(0, shards, fill_send, 0)

    owners = [lax.div(source_ref[me * blocks + i], blocks) for i in range(blocks)]
    for i in range(blocks):
        rank = jnp.int32(0)
        for j in range(i):
            rank = rank + jnp.where(owners[j] == owners[i], 1, 0)
        take_table[i] = owners[i] * cap + rank

    def fill_reach(i, carry):
        block = me * blocks + i
        mine = doc_ref[block]
        count = jnp.int32(0)
        for back in range(1, DOCMAX):
            other = doc_ref[jnp.maximum(block - back, 0)]
            count = count + jnp.where((block - back >= 0) & (other == mine), 1, 0)
        reach_table[i] = (REACH - count) * BLK
        return carry

    lax.fori_loop(0, blocks, fill_reach, 0)

    pl.semaphore_wait(barrier, shards - 1 + groups - 1)

    def send_copy(unit, shard):
        return pltpu.make_async_remote_copy(
            src_ref=outgoing[unit].at[pl.ds(shard * cap, cap)],
            dst_ref=incoming[unit].at[pl.ds(me * cap, cap)],
            send_sem=send_sem.at[unit, shard],
            recv_sem=recv_sem.at[unit, me],
            device_id={"ctx": shard},
            device_id_type=pl.DeviceIdType.MESH,
        )

    def arrival(unit, shard):
        return pltpu.make_async_remote_copy(
            src_ref=outgoing[unit].at[pl.ds(shard * cap, cap)],
            dst_ref=incoming[unit].at[pl.ds(shard * cap, cap)],
            send_sem=send_sem.at[unit, shard],
            recv_sem=recv_sem.at[unit, shard],
            device_id={"ctx": shard},
            device_id_type=pl.DeviceIdType.MESH,
        )

    def own_copy(unit):
        return pltpu.make_async_copy(
            outgoing[unit].at[pl.ds(me * cap, cap)],
            incoming[unit].at[pl.ds(me * cap, cap)],
            own_sem.at[unit],
        )

    def start_unit(unit):
        load(unit).wait()

        def gather(step, carry):
            shard = lax.rem(me + step, shards)
            for r in range(cap):
                slot = shard * cap + r
                outgoing[unit][slot] = local[unit][send_table[slot]]

            @pl.when(step < shards)
            def _():
                send_copy(unit, shard).start()

            return carry

        lax.fori_loop(1, shards + 1, gather, 0)
        own_copy(unit).start()

    def await_unit(unit):
        own_copy(unit).wait()

        def wait(step, carry):
            arrival(unit, lax.rem(me + step, shards)).wait_recv()
            return carry

        lax.fori_loop(1, shards, wait, 0)

    def await_sent(unit):
        def wait(step, carry):
            send_copy(unit, lax.rem(me + step, shards)).wait_send()
            return carry

        lax.fori_loop(1, shards, wait, 0)

    for unit in range(min(2 + LOOKAHEAD, units)):
        start_unit(unit)

    def shift_copy(index, ext, direction):
        return pltpu.make_async_remote_copy(
            src_ref=ext.at[:, pl.ds(blocks, REACH)],
            dst_ref=ext.at[:, pl.ds(0, REACH)],
            send_sem=shift_send.at[index],
            recv_sem=shift_recv.at[index],
            device_id={"ctx": me + direction},
            device_id_type=pl.DeviceIdType.MESH,
        )

    for index, ext in enumerate((key_ext, value_ext)):
        await_unit(index)

        def assemble(i, carry):
            block = incoming[index][take_table[i]]
            for h in range(kv_heads):
                ext[h, REACH + i] = block[:, h * HEAD_SIZE:(h + 1) * HEAD_SIZE]
            return carry

        lax.fori_loop(0, blocks, assemble, 0)

        @pl.when(me < shards - 1)
        def _():
            shift_copy(index, ext, 1).start()

        @pl.when(me == 0)
        def _():
            ext[:, 0:REACH] = jnp.zeros((kv_heads, REACH, BLK, HEAD_SIZE), ext.dtype)

    for index, ext in enumerate((key_ext, value_ext)):
        @pl.when(me > 0)
        def _():
            shift_copy(index, ext, -1).wait_recv()

    def out_copy(chunk, group):
        return pltpu.make_async_remote_copy(
            src_ref=result.at[chunk, group],
            dst_ref=out.at[:, :, pl.ds(my_group * (chunks * width) + chunk * width, width)],
            send_sem=out_send.at[chunk, group],
            recv_sem=out_recv.at[chunk, my_group],
            device_id={"head": group},
            device_id_type=pl.DeviceIdType.MESH,
        )

    def out_arrival(chunk, group):
        return pltpu.make_async_remote_copy(
            src_ref=result.at[chunk, group],
            dst_ref=out.at[:, :, pl.ds(group * (chunks * width) + chunk * width, width)],
            send_sem=out_send.at[chunk, group],
            recv_sem=out_recv.at[chunk, group],
            device_id={"head": group},
            device_id_type=pl.DeviceIdType.MESH,
        )

    def out_own(chunk):
        return pltpu.make_async_copy(
            result.at[chunk, my_group],
            out.at[:, :, pl.ds(my_group * (chunks * width) + chunk * width, width)],
            out_send.at[chunk, my_group],
        )

    heads = width // HEAD_SIZE
    rows = heads * BLK
    window = DOCMAX * BLK
    factor = HEAD_SIZE ** -0.5 * LOG2E

    def group_at(step):
        chips = groups // 2
        chip, core = my_group // 2, lax.rem(my_group, 2)
        return (lax.rem(chip + chips - 1 - step // 2 + chips, chips) * 2
                + lax.rem(core + 1 + step, 2))

    def one_chunk(chunk, carry):
        for k in range(chunks):
            @pl.when(chunk == k)
            def _():
                await_unit(2 + k)
                if 2 + k + LOOKAHEAD < units:
                    start_unit(2 + k + LOOKAHEAD)

                def move(i, inner):
                    stage[i] = incoming[2 + k][take_table[i]]
                    return inner

                lax.fori_loop(0, blocks, move, 0)

        kv = (chunk * heads) // group_size

        def one_group(step, inner):
            group = group_at(step)

            def one_block(j, deep):
                block = group * quarter + j
                query = stage[block]
                query = jnp.concatenate(
                    [query[:, h * HEAD_SIZE:(h + 1) * HEAD_SIZE] for h in range(heads)], axis=0)
                key = key_ext[kv, pl.ds(block, DOCMAX)].reshape(window, HEAD_SIZE)
                value = value_ext[kv, pl.ds(block, DOCMAX)].reshape(window, HEAD_SIZE)
                scores = lax.dot_general(query, key, (((1,), (1,)), ((), ())),
                                         preferred_element_type=jnp.float32)
                column = lax.broadcasted_iota(jnp.int32, (rows, window), 1)
                row = lax.rem(lax.broadcasted_iota(jnp.int32, (rows, window), 0), BLK)
                allowed = (column >= reach_table[block]) & (column <= row + REACH * BLK)
                scores = jnp.where(allowed, scores, -1e30)
                top = jnp.max(scores, axis=1, keepdims=True)
                terms = jnp.exp2((scores - top) * factor)
                total = jnp.sum(terms, axis=1, keepdims=True)
                mixed = jnp.dot(terms.astype(jnp.bfloat16), value,
                                preferred_element_type=jnp.float32)
                mixed = (mixed / total).astype(jnp.bfloat16)
                for h in range(heads):
                    result[chunk, group, j, :, h * HEAD_SIZE:(h + 1) * HEAD_SIZE] = (
                        mixed[h * BLK:(h + 1) * BLK])
                return deep

            lax.fori_loop(0, quarter, one_block, 0)

            @pl.when(step < groups - 1)
            def _():
                out_copy(chunk, group).start()

            @pl.when(step == groups - 1)
            def _():
                out_own(chunk).start()

            return inner

        lax.fori_loop(0, groups, one_group, 0)
        return carry

    lax.fori_loop(0, chunks, one_chunk, 0)

    for unit in range(units):
        await_sent(unit)

    for index, ext in enumerate((key_ext, value_ext)):
        @pl.when(me < shards - 1)
        def _():
            shift_copy(index, ext, 1).wait_send()

    def finish(chunk, carry):
        out_own(chunk).wait()

        def wait(step, inner):
            group = lax.rem(my_group + step, groups)
            out_copy(chunk, group).wait_send()
            out_arrival(chunk, group).wait_recv()
            return inner

        lax.fori_loop(1, groups, wait, 0)
        return carry

    lax.fori_loop(0, chunks, finish, 0)


def local(queries, keys, values, source_block, doc_of_block):
    shards = lax.axis_size("ctx")
    groups = lax.axis_size("head")
    row_count, query_width = queries.shape
    kv_width = keys.shape[1]
    blocks = row_count // BLK
    cap = max(1, blocks // shards)
    kv_heads = kv_width // HEAD_SIZE
    group_size = query_width // kv_width
    width = HEADS_PER_CHUNK * HEAD_SIZE
    chunks = query_width // width
    units = 2 + chunks
    quarter = blocks // groups
    dims = (shards, groups, blocks, cap, kv_heads, chunks, width, kv_width, group_size)
    kind = queries.dtype
    widths = [kv_width, kv_width] + [width] * chunks
    anywhere = pl.BlockSpec(memory_space=pl.ANY)
    scalars = pl.BlockSpec(memory_space=pltpu.SMEM)
    dma = pltpu.SemaphoreType.DMA
    out = pl.pallas_call(
        functools.partial(kernel, dims),
        out_shape=jax.ShapeDtypeStruct((quarter, BLK, groups * query_width), kind),
        in_specs=[scalars, scalars, anywhere, anywhere, anywhere],
        out_specs=anywhere,
        scratch_shapes=(
            [pltpu.VMEM((blocks, BLK, w), kind) for w in widths]
            + [pltpu.VMEM((shards * cap, BLK, w), kind) for w in widths]
            + [pltpu.VMEM((shards * cap, BLK, w), kind) for w in widths]
            + [pltpu.VMEM((kv_heads, REACH + blocks, BLK, HEAD_SIZE), kind)] * 2
            + [
                pltpu.VMEM((blocks, BLK, width), kind),
                pltpu.VMEM((chunks, groups, quarter, BLK, width), kind),
                pltpu.SMEM((shards * cap,), jnp.int32),
                pltpu.SMEM((blocks,), jnp.int32),
                pltpu.SMEM((blocks,), jnp.int32),
                dma((units,)),
                dma((units,)),
                dma((units, shards)),
                dma((units, shards)),
                dma((2,)),
                dma((2,)),
                dma((chunks, groups)),
                dma((chunks, groups)),
            ]
        ),
        compiler_params=pltpu.CompilerParams(
            collective_id=0, has_side_effects=True, vmem_limit_bytes=58 * 1024 * 1024
        ),
    )(
        source_block,
        doc_of_block,
        queries.reshape(blocks, BLK, query_width),
        keys.reshape(blocks, BLK, kv_width),
        values.reshape(blocks, BLK, kv_width),
    )
    return out.reshape(row_count // groups, groups * query_width)


def solution(mesh):
    in_specs = (P("ctx", "head"), P("ctx", "head"), P("ctx", "head"), P(), P())
    out_specs = P(("ctx", "head"), None)
    return jax.shard_map(local, mesh=mesh, in_specs=in_specs, out_specs=out_specs, check_vma=False)
```

time: 799 us -> 277 us (0.35)
  Pallas kernels: 0 us -> 269 us
  waiting for transfers between devices: 186 us -> 0 us
  matrix products: 158 us -> 0 us
  local copies, waits for them, and re-layouts: 141 us -> 7.77 us
  blocking collectives: 130 us -> 0 us
  other arithmetic: 113 us -> 0 us
  loops' own time: 45.2 us -> 0 us
  starting transfers between devices: 18.7 us -> 0 us
    pallas_call x0 -> x1, Pallas kernels: none -> 269 us  [local(): pl.pallas_call(functools.partial(kernel, dims), out_shape=jax.ShapeDtypeS...]
    ppermute x2 -> x0, waiting for transfers between devices: 186 us -> none  [shifted(): return lax.ppermute(block, axis, route)]
    all_to_all x2 -> x0, blocking collectives: 130 us -> none  [the longest x1 101 us: local(): lax.all_to_all(flattened, 'head', split_axis=0, concat_axis=1, tiled=True)]
    sub x16 -> x0, matrix products: 88.4 us -> none  [one_block(): expo_terms = jnp.where(allowed, jnp.exp(masked - row_max), 0.0)]
    gather x51 -> x0, other arithmetic: 78.5 us -> none  [the longest x48 78.5 us: one_block(): allowed = causal & same_doc[key_pos // BLK][None, :]]
    dot_general x16 -> x0, matrix products: 70 us -> none  [one_block(): jnp.einsum('ngqk,knd->qngd', weights, value_window, preferred_element_typ...]
    another operation x1 -> x0, loops' own time: 45.2 us -> none  [attend(): stacked = lax.map(one_block, jnp.arange(block_total, dtype=jnp.int32))]
    all_to_all x3 -> x0, local copies, waits for them, and re-layouts: 36.6 us -> none  [local(): lax.all_to_all(flattened, 'head', split_axis=0, concat_axis=1, tiled=True)]
  transfers between devices with their start and end apart: 4 -> 0, of which waited for: 2 -> 0; matrix products, arithmetic and copies ran while one was open for 4% -> 0% of each run, Pallas kernels for 0% -> 0%
where the time goes in v1:
time: 277 us
  Pallas kernels  269 us (97%)
  local copies, waits for them, and re-layouts  7.77 us (3%)
    pallas_call x1, Pallas kernels, local(): pl.pallas_call(functools.partial(kernel, dims), out_shape=jax.ShapeDtypeS...  269 us
    unnamed x1, local copies, waits for them, and re-layouts  7.77 us

profile of v1, /device:TPU:12, one launch (start us, length us, event | category | flops | bytes accessed | tf_op | source)
XLA Modules:
  0.0 277.0 jit_solution(4082156541306028313)
XLA Ops:
  0.0 269.3 %shard_map.55 = bf16[4,128,8192]{2,1,0:T(8,128)(2,1)} custom-call(s32[128]{0:T(128)} %source_ref.1, s32[128]{0:T(128)} %doc_ref.1, bf16[16,128,2048]{2,1,0:T(8,128)(2,1)} %bitcast.5, bf16[16,128,256]{2,1,0:T(8,128)(2,1)} %bitcast.6, bf16[16,128,256]{2,1,0:T(8,128)(2,1)} %bitcast.7), custom_call_target="tpu_custom_call" | custom-call | tf_op jit(solution)/shard_map/pallas_call | solution.py:341
  269.3 7.8 %copy.7 = bf16[512,8192]{1,0:T(8,128)(2,1)} copy(bf16[512,8192]{1,0:T(8,128)(2,1)} %bitcast.4) | data formatting | bytes 16777216

commit v2 on v1

--- a/solution.py
+++ b/solution.py
@@ -29,8 +29,9 @@
     local = take(units)
     outgoing = take(units)
     incoming = take(units)
-    (key_ext, value_ext, stage, result, send_table, take_table, reach_table) = take(7)
-    (load_sem, own_sem, send_sem, recv_sem, shift_send, shift_recv, out_send, out_recv) = take(8)
+    (key_ext, value_ext, relay, stage, result, send_table, take_table, reach_table) = take(8)
+    (load_sem, own_sem, send_sem, recv_sem, shift_send, shift_recv, relay_sem,
+     out_send, out_recv) = take(9)
 
     me = lax.axis_index("ctx")
     my_group = lax.axis_index("head")
@@ -79,6 +80,72 @@
 
     lax.fori_loop(0, shards, fill_send, 0)
 
+    pl.semaphore_wait(barrier, shards - 1 + groups - 1)
+
+    def send_copy(unit, shard):
+        return pltpu.make_async_remote_copy(
+            src_ref=outgoing[unit].at[pl.ds(shard * cap, cap)],
+            dst_ref=incoming[unit].at[pl.ds(me * cap, cap)],
+            send_sem=send_sem.at[unit, shard],
+            recv_sem=recv_sem.at[unit, me],
+            device_id={"ctx": shard},
+            device_id_type=pl.DeviceIdType.MESH,
+        )
+
+    def arrival(unit, shard):
+        return pltpu.make_async_remote_copy(
+            src_ref=outgoing[unit].at[pl.ds(shard * cap, cap)],
+            dst_ref=incoming[unit].at[pl.ds(shard * cap, cap)],
+            send_sem=send_sem.at[unit, shard],
+            recv_sem=recv_sem.at[unit, shard],
+            device_id={"ctx": shard},
+            device_id_type=pl.DeviceIdType.MESH,
+        )
+
+    def own_copy(unit):
+        return pltpu.make_async_copy(
+            outgoing[unit].at[pl.ds(me * cap, cap)],
+            incoming[unit].at[pl.ds(me * cap, cap)],
+            own_sem.at[unit],
+        )
+
+    def start_unit(unit):
+        load(unit).wait()
+
+        def gather(step, carry):
+            shard = lax.rem(me + step, shards)
+            for r in range(cap):
+                slot = shard * cap + r
+                outgoing[unit][slot] = local[unit][send_table[slot]]
+
+            @pl.when(step < shards)
+            def _():
+                send_copy(unit, shard).start()
+
+            return carry
+
+        lax.fori_loop(1, shards + 1, gather, 0)
+        own_copy(unit).start()
+
+    def await_unit(unit):
+        own_copy(unit).wait()
+
+        def wait(step, carry):
+            arrival(unit, lax.rem(me + step, shards)).wait_recv()
+            return carry
+
+        lax.fori_loop(1, shards, wait, 0)
+
+    def await_sent(unit):
+        def wait(step, carry):
+            send_copy(unit, lax.rem(me + step, shards)).wait_send()
+            return carry
+
+        lax.fori_loop(1, shards, wait, 0)
+
+    for unit in range(min(2 + LOOKAHEAD, units)):
+        start_unit(unit)
+
     owners = [lax.div(source_ref[me * blocks + i], blocks) for i in range(blocks)]
     for i in range(blocks):
         rank = jnp.int32(0)
@@ -98,72 +165,6 @@
 
     lax.fori_loop(0, blocks, fill_reach, 0)
 
-    pl.semaphore_wait(barrier, shards - 1 + groups - 1)
-
-    def send_copy(unit, shard):
-        return pltpu.make_async_remote_copy(
-            src_ref=outgoing[unit].at[pl.ds(shard * cap, cap)],
-            dst_ref=incoming[unit].at[pl.ds(me * cap, cap)],
-            send_sem=send_sem.at[unit, shard],
-            recv_sem=recv_sem.at[unit, me],
-            device_id={"ctx": shard},
-            device_id_type=pl.DeviceIdType.MESH,
-        )
-
-    def arrival(unit, shard):
-        return pltpu.make_async_remote_copy(
-            src_ref=outgoing[unit].at[pl.ds(shard * cap, cap)],
-            dst_ref=incoming[unit].at[pl.ds(shard * cap, cap)],
-            send_sem=send_sem.at[unit, shard],
-            recv_sem=recv_sem.at[unit, shard],
-            device_id={"ctx": shard},
-            device_id_type=pl.DeviceIdType.MESH,
-        )
-
-    def own_copy(unit):
-        return pltpu.make_async_copy(
-            outgoing[unit].at[pl.ds(me * cap, cap)],
-            incoming[unit].at[pl.ds(me * cap, cap)],
-            own_sem.at[unit],
-        )
-
-    def start_unit(unit):
-        load(unit).wait()
-
-        def gather(step, carry):
-            shard = lax.rem(me + step, shards)
-            for r in range(cap):
-                slot = shard * cap + r
-                outgoing[unit][slot] = local[unit][send_table[slot]]
-
-            @pl.when(step < shards)
-            def _():
-                send_copy(unit, shard).start()
-
-            return carry
-
-        lax.fori_loop(1, shards + 1, gather, 0)
-        own_copy(unit).start()
-
-    def await_unit(unit):
-        own_copy(unit).wait()
-
-        def wait(step, carry):
-            arrival(unit, lax.rem(me + step, shards)).wait_recv()
-            return carry
-
-        lax.fori_loop(1, shards, wait, 0)
-
-    def await_sent(unit):
-        def wait(step, carry):
-            send_copy(unit, lax.rem(me + step, shards)).wait_send()
-            return carry
-
-        lax.fori_loop(1, shards, wait, 0)
-
-    for unit in range(min(2 + LOOKAHEAD, units)):
-        start_unit(unit)
-
     def shift_copy(index, ext, direction):
         return pltpu.make_async_remote_copy(
             src_ref=ext.at[:, pl.ds(blocks, REACH)],
@@ -174,6 +175,30 @@
             device_id_type=pl.DeviceIdType.MESH,
         )
 
+    first_hop, second_hop = -1, 2
+    relays = (me % 2 == 1) & (me < shards - 1)
+    forwards = ((me - first_hop) % 2 == 1) & (me - first_hop > 0) & (me - first_hop < shards - 1)
+
+    def relay_copy():
+        return pltpu.make_async_remote_copy(
+            src_ref=value_ext.at[:, pl.ds(blocks, REACH)],
+            dst_ref=relay,
+            send_sem=relay_sem.at[0],
+            recv_sem=relay_sem.at[1],
+            device_id={"ctx": me + first_hop},
+            device_id_type=pl.DeviceIdType.MESH,
+        )
+
+    def forward_copy():
+        return pltpu.make_async_remote_copy(
+            src_ref=relay,
+            dst_ref=value_ext.at[:, pl.ds(0, REACH)],
+            send_sem=relay_sem.at[2],
+            recv_sem=shift_recv.at[1],
+            device_id={"ctx": me + second_hop},
+            device_id_type=pl.DeviceIdType.MESH,
+        )
+
     for index, ext in enumerate((key_ext, value_ext)):
         await_unit(index)
 
@@ -185,13 +210,24 @@
 
         lax.fori_loop(0, blocks, assemble, 0)
 
-        @pl.when(me < shards - 1)
+        straight = (me < shards - 1) if index == 0 else (me < shards - 1) & (me % 2 == 0)
+
+        @pl.when(straight)
         def _():
             shift_copy(index, ext, 1).start()
 
         @pl.when(me == 0)
         def _():
             ext[:, 0:REACH] = jnp.zeros((kv_heads, REACH, BLK, HEAD_SIZE), ext.dtype)
+
+    @pl.when(relays)
+    def _():
+        relay_copy().start()
+
+    @pl.when(forwards)
+    def _():
+        relay_copy().wait_recv()
+        forward_copy().start()
 
     for index, ext in enumerate((key_ext, value_ext)):
         @pl.when(me > 0)
@@ -300,9 +336,19 @@
         await_sent(unit)
 
     for index, ext in enumerate((key_ext, value_ext)):
-        @pl.when(me < shards - 1)
+        straight = (me < shards - 1) if index == 0 else (me < shards - 1) & (me % 2 == 0)
+
+        @pl.when(straight)
         def _():
             shift_copy(index, ext, 1).wait_send()
+
+    @pl.when(relays)
+    def _():
+        relay_copy().wait_send()
+
+    @pl.when(forwards)
+    def _():
+        forward_copy().wait_send()
 
     def finish(chunk, carry):
         out_own(chunk).wait()
@@ -349,6 +395,7 @@
             + [pltpu.VMEM((shards * cap, BLK, w), kind) for w in widths]
             + [pltpu.VMEM((kv_heads, REACH + blocks, BLK, HEAD_SIZE), kind)] * 2
             + [
+                pltpu.VMEM((kv_heads, REACH, BLK, HEAD_SIZE), kind),
                 pltpu.VMEM((blocks, BLK, width), kind),
                 pltpu.VMEM((chunks, groups, quarter, BLK, width), kind),
                 pltpu.SMEM((shards * cap,), jnp.int32),
@@ -360,6 +407,7 @@
                 dma((units, shards)),
                 dma((2,)),
                 dma((2,)),
+                dma((3,)),
                 dma((chunks, groups)),
                 dma((chunks, groups)),
             ]

time: 277 us -> 268 us (0.968)
  Pallas kernels: 269 us -> 259 us
    pallas_call x1, Pallas kernels: 269 us -> 259 us  [local(): pl.pallas_call(functools.partial(kernel, dims), out_shape=jax.ShapeDtypeS...]
where the time goes in v2:
time: 268 us; the launch traced here: 267 us
  Pallas kernels  259 us (97%)
  local copies, waits for them, and re-layouts  7.77 us (3%)
    pallas_call x1, Pallas kernels, local(): pl.pallas_call(functools.partial(kernel, dims), out_shape=jax.ShapeDtypeS...  259 us
    unnamed x1, local copies, waits for them, and re-layouts  7.77 us

profile of v2, /device:TPU:12, one launch (start us, length us, event | category | flops | bytes accessed | tf_op | source)
XLA Modules:
  0.0 266.6 jit_solution(6039542598213760743)
XLA Ops:
  0.0 258.8 %shard_map.55 = bf16[4,128,8192]{2,1,0:T(8,128)(2,1)} custom-call(s32[128]{0:T(128)} %source_ref.1, s32[128]{0:T(128)} %doc_ref.1, bf16[16,128,2048]{2,1,0:T(8,128)(2,1)} %bitcast.5, bf16[16,128,256]{2,1,0:T(8,128)(2,1)} %bitcast.6, bf16[16,128,256]{2,1,0:T(8,128)(2,1)} %bitcast.7), custom_call_target="tpu_custom_call" | custom-call | tf_op jit(solution)/shard_map/pallas_call | solution.py:387
  258.8 7.8 %copy.7 = bf16[512,8192]{1,0:T(8,128)(2,1)} copy(bf16[512,8192]{1,0:T(8,128)(2,1)} %bitcast.4) | data formatting | bytes 16777216
